TPU v7x, 32 devices: a whole 2x2x4 slice. The times are simulated.
32 devices in a mesh: dp: 8 (over z, x), feat: 4 (over y, core).
Axes of the slice: x: 2, y: 2, z: 4, core: 2. Of those that a mesh axis runs over, the one named last changes fastest.
Arguments:
- samples: bfloat16 [8192, 1024], P('dp', 'feat'), may hold values from -6 to 6
- freqs: bfloat16 [1024, 32768], P('dp', 'feat'), may hold values from -0.1875 to 0.1875
- phases: float32 [32768], P('feat'), may hold values from -3.140625 to 3.140625
- range_test: bfloat16 [32768, 256], P('feat'), may hold values from -6 to 6
- corange_test: bfloat16 [256, 8192], P(None, 'dp'), may hold values from -6 to 6
Outputs:
- range_sketch: float32 [8192, 256], P(('dp', 'feat'))
- corange_sketch: float32 [256, 32768], P('dp', 'feat')
All inputs are finite; a program needn't handle non-finite values.
Results may differ from a plain program's by a relative error of at most 0.0024.
Values may be sent and summed in bfloat16 or wider, within the bound.
A program may use at most 128 MiB of HBM per device.

v0:
```python
import math

import jax
import jax.numpy as jnp
from jax import lax
from jax.sharding import PartitionSpec as P


def on_device(samples, freqs, phases, range_test, corange_test):
    gathered = lax.all_gather(samples, "feat", axis=1, tiled=True)
    feature_count = freqs.shape[1]
    projection = jnp.dot(
        gathered,
        lax.all_gather(freqs, "dp", axis=0, tiled=True),
        preferred_element_type=jnp.float32,
    )
    scale = math.sqrt(2.0 / (feature_count * lax.axis_size("feat")))
    features = (scale * jnp.cos(projection + phases[None, :])).astype(jnp.bfloat16)
    range_sketch = lax.psum_scatter(
        jnp.dot(features, range_test, preferred_element_type=jnp.float32),
        "feat",
        scatter_dimension=0,
        tiled=True,
    )
    corange_sketch = lax.psum_scatter(
        jnp.dot(corange_test, features, preferred_element_type=jnp.float32),
        "dp",
        scatter_dimension=0,
        tiled=True,
    )
    return (range_sketch, corange_sketch)


def solution(mesh):
    placed = (P("dp", "feat"), P("dp", "feat"), P("feat"), P("feat", None), P(None, "dp"))
    return jax.shard_map(
        on_device,
        mesh=mesh,
        in_specs=placed,
        out_specs=(P(("dp", "feat"), None), P("dp", "feat")),
        check_vma=False,
    )
```

profile of v0, /device:TPU:26, one launch (start us, length us, event | category | flops | bytes accessed | tf_op | source)
XLA Modules:
  0.0 579.8 jit_solution(11586309907684146967)
XLA Ops:
  7.2 0.0 copy-start
  7.2 0.0 all-gather.3.cloned.1.call-start
  7.2 0.7 all-gather.3.cloned.1.call-update
  7.9 0.0 all-gather.5.cloned.1.call-start
  8.0 0.7 all-gather.5.cloned.1.call-update
  8.7 0.0 reduce-scatter.5.cloned.1.call-start
  8.7 24.7 %all-gather.3.cloned.1.call-done = bf16[1024,1024]{1,0:T(8,128)(2,1)} async-done(((bf16[1024,256]{1,0:T(8,128)(2,1)}), bf16[1024,1024]{1,0:T(8,128)(2,1)}) %all-gather.3.cloned.1.call-update) | async-done | bytes 2097168 | tf_op jit(solution)/shard_map/all_gather | solution.py:10
  33.4 226.8 %all-gather.5.cloned.1.call-done = bf16[1024,8192]{1,0:T(8,128)(2,1)} async-done(((bf16[128,8192]{1,0:T(8,128)(2,1)}), bf16[1024,8192]{1,0:T(8,128)(2,1)}) %all-gather.5.cloned.1.call-update) | async-done | bytes 16777232 | tf_op jit(solution)/shard_map/all_gather | solution.py:14
  260.2 0.0 copy-start.1
  260.2 124.0 %multiply_convert_fusion = bf16[1024,8192]{1,0:T(8,128)(2,1)S(1)} fusion(bf16[1024,1024]{1,0:T(8,128)(2,1)} %all-gather.3.cloned.1.call-done, bf16[1024,8192]{1,0:T(8,128)(2,1)} %all-gather.5.cloned.1.call-done, f32[8192]{0:T(1024)} %param.7), kind=kOutput, calls=%fused_computation | convolution fusion | flops 17205035008 | bytes 35684352 | tf_op jit(solution)/shard_map/dot_general | solution.py:12
  384.2 0.0 copy-start.2
  384.2 5.7 copy-done.2
  390.0 0.0 copy-done.1
  390.0 5.5 fusion
  395.5 0.0 reduce-scatter.5.cloned.1.call-update
  395.5 0.0 reduce-scatter.7.cloned.1.call-start
  395.6 0.0 copy-done
  395.6 13.7 %convolution_bitcast_fusion = f32[256,8192]{0,1:T(8,128)} fusion(bf16[1024,8192]{1,0:T(8,128)(2,1)} %copy-done.2, bf16[256,1024]{1,0:T(8,128)(2,1)S(1)} %copy-done), kind=kOutput, calls=%fused_computation.1 | convolution fusion | flops 4294967296 | bytes 25690112 | tf_op jit(solution)/shard_map/dot_general | solution.py:26
  409.3 9.0 %copy.9 = f32[256,8192]{1,0:T(8,128)} copy(f32[256,8192]{0,1:T(8,128)} %convolution_bitcast_fusion) | data formatting | bytes 16777216
  418.3 0.0 reduce-scatter.7.cloned.1.call-update
  418.3 3.3 reduce-scatter.5.cloned.1.call-done
  421.7 151.6 %reduce-scatter.7.cloned.1.call-done = f32[32,8192]{1,0:T(8,128)} async-done(((f32[256,8192]{1,0:T(8,128)}), f32[32,8192]{1,0:T(8,128)}) %reduce-scatter.7.cloned.1.call-update) | async-done | bytes 1048592
Async XLA Ops:
  7.2 388.4 %copy-start = (bf16[256,1024]{1,0:T(8,128)(2,1)S(1)}, bf16[256,1024]{1,0:T(8,128)(2,1)}, u32[]{:S(2)}) copy-start(bf16[256,1024]{1,0:T(8,128)(2,1)} %param.9) | copy-start | bytes 1572868
  7.2 26.2 %all-gather.3.cloned.1.call-start = ((), (), s32[]{:S(2)}) async-start(), calls=%async_computation.2 | async-start | bytes 2621440 | tf_op jit(solution)/shard_map/all_gather | solution.py:10
  7.9 252.3 %all-gather.5.cloned.1.call-start = ((), (), s32[]{:S(2)}) async-start(), calls=%async_computation.3 | async-start | bytes 18874368 | tf_op jit(solution)/shard_map/all_gather | solution.py:14
  8.7 413.0 %reduce-scatter.5.cloned.1.call-start = ((), (), s32[]{:S(2)}) async-start(), calls=%async_computation.4 | async-start | bytes 1310720 | tf_op jit(solution)/shard_map/reduce_scatter | solution.py:19
  260.2 129.7 %copy-start.1 = (bf16[8192,256]{1,0:T(8,128)(2,1)S(1)}, bf16[8192,256]{1,0:T(8,128)(2,1)}, u32[]{:S(2)}) copy-start(bf16[8192,256]{1,0:T(8,128)(2,1)} %param.8) | copy-start | bytes 12582916
  384.2 5.7 copy-start.2
  395.5 177.8 %reduce-scatter.7.cloned.1.call-start = ((), (), s32[]{:S(2)}) async-start(), calls=%async_computation.5 | async-start | bytes 9437184
Sparse Core Ops, SparseCore 0:
  9.6 23.7 all-gather.2
  35.5 224.6 all-gather.4
  395.7 25.9 reduce-scatter.4
  426.2 147.0 reduce-scatter.6
where the time goes:
time: 584 us; the launch traced here: 580 us
  waiting for transfers between devices  408 us (70%)
  matrix products  143 us (24%)
  local copies, waits for them, and re-layouts  14.7 us (3%)
  between operations  13.8 us (2%)
    all_gather x1, waiting for transfers between devices, on_device(): lax.all_gather(freqs, 'dp', axis=0, tiled=True)  227 us
    unnamed x5, waiting for transfers between devices  153 us
    dot_general x1, matrix products, on_device(): jnp.dot(gathered, lax.all_gather(freqs, 'dp', axis=0, tiled=True), prefer...  124 us
    all_gather x1, waiting for transfers between devices, on_device(): gathered = lax.all_gather(samples, 'feat', axis=1, tiled=True)  24.7 us
    unnamed x7, local copies, waits for them, and re-layouts  14.7 us
    dot_general x1, matrix products, on_device(): jnp.dot(corange_test, features, preferred_element_type=jnp.float32)  13.7 us
  transfers between devices with their start and end apart: 4, of which 4 were waited for; matrix products, arithmetic and copies ran while one was open for 4% of the time, Pallas kernels for 0%

commit v1 on v0

v1 whole, which is shorter than its diff:
```python
import functools
import math

import jax
import jax.numpy as jnp
from jax import lax
from jax.experimental import pallas as pl
from jax.experimental.pallas import tpu as pltpu
from jax.sharding import PartitionSpec as P

MESH = pl.DeviceIdType.MESH
INV_TURN = 1.0 / (2.0 * math.pi)
SIN_TURN = (6.283164044278293, -41.33714236799647, 81.34076878818043, -70.99343236149275)
WIRE = jnp.float32
LANES = 128


def scaled_cos(turns, scale):
    nearest = lax.round(turns, lax.RoundingMethod.TO_NEAREST_EVEN)
    g = 0.25 - jnp.abs(turns - nearest)
    s = g * g
    poly = jnp.float32(SIN_TURN[-1] * scale)
    for coef in SIN_TURN[-2::-1]:
        poly = poly * s + jnp.float32(coef * scale)
    return poly * g


def kernel(
    groups, scale,
    s_in, w_in, ph_in, rt_in, ct_in,
    out_r, out_c,
    S, W, PH, RT, CT, R, C, RC, RY, RZ, RS, RF, CX, CS, CR,
    local_sem, w_send, w_recv, s_send, s_recv, t_send, t_recv,
    rc_send, rc_recv, ry_send, ry_recv, rz_send, rz_recv,
    cx_send, cx_recv, cz_send, cz_recv,
):
    G = groups
    d, f = lax.axis_index("dp"), lax.axis_index("feat")
    z, x = d // 2, d % 2
    y, c = f // 2, f % 2
    fy, fc = (1 - y) * 2 + c, y * 2 + (1 - c)
    dx = z * 2 + (1 - x)
    x_peer, y_peer, c_peer = (dx, f), (d, fy), (d, fc)

    rows, width = s_in.shape
    depth = w_in.shape[0]
    cols = w_in.shape[1] // G
    rank = ct_in.shape[0]
    t_rows = rank // 4
    c_rows = rank // (2 * G)
    r_rows = rows // 4

    def zid(j):
        return (z + j) % G

    def z_peer(j):
        return (zid(j) * 2 + x, f)

    barrier = pltpu.get_barrier_semaphore()
    peers = [z_peer(j) for j in range(1, G)] + [x_peer, y_peer, c_peer]
    for peer in peers:
        pl.semaphore_signal(barrier, inc=1, device_id=peer, device_id_type=MESH)

    def w_block(who):
        return W.at[pl.ds(pl.multiple_of(who * depth, depth), depth), :]

    def s_block(zz, ff):
        return S.at[
            pl.ds(pl.multiple_of(zz * rows, rows), rows),
            pl.ds(pl.multiple_of(ff * width, LANES), width),
        ]

    def t_block(zz, ff):
        return CT.at[
            pl.ds(pl.multiple_of(ff * t_rows, t_rows), t_rows),
            pl.ds(pl.multiple_of(zz * rows, LANES), rows),
        ]

    def w_cols(zz):
        return w_in.at[:, pl.ds(pl.multiple_of(zz * cols, LANES), cols)]

    own_t = ct_in.at[pl.ds(pl.multiple_of(f * t_rows, t_rows), t_rows), :]
    col0 = pl.multiple_of(z * cols, LANES)

    locals_ = [
        pltpu.make_async_copy(w_cols(z), w_block(d), local_sem.at[0]),
        pltpu.make_async_copy(s_in, s_block(z, f), local_sem.at[1]),
        pltpu.make_async_copy(own_t, t_block(z, f), local_sem.at[2]),
        pltpu.make_async_copy(rt_in.at[pl.ds(col0, cols), :], RT, local_sem.at[3]),
        pltpu.make_async_copy(ph_in.at[:, pl.ds(col0, cols)], PH, local_sem.at[4]),
    ]
    for copy in locals_:
        copy.start()

    started = []

    def send(src, dst, ssem, rsem, peer):
        copy = pltpu.make_async_remote_copy(
            src_ref=src, dst_ref=dst, send_sem=ssem, recv_sem=rsem,
            device_id=peer, device_id_type=MESH,
        )
        copy.start()
        started.append(copy)

    def arrive(dst, ssem, rsem):
        pltpu.make_async_remote_copy(
            src_ref=dst, dst_ref=dst, send_sem=ssem, recv_sem=rsem,
            device_id=x_peer, device_id_type=MESH,
        ).wait_recv()

    counts = {"s": 0}

    def send_st(s_src, t_src, zz, ff, peer):
        n = counts["s"]
        counts["s"] = n + 1
        index = zz * 4 + ff
        send(s_src, s_block(zz, ff), s_send.at[n], s_recv.at[index], peer)
        send(t_src, t_block(zz, ff), t_send.at[n], t_recv.at[index], peer)

    def arrive_st(zz, ff):
        index = zz * 4 + ff
        arrive(s_block(zz, ff), s_send.at[0], s_recv.at[index])
        arrive(t_block(zz, ff), t_send.at[0], t_recv.at[index])

    pl.semaphore_wait(barrier, len(peers))

    for j in range(G - 1, 0, -1):
        send(w_cols(zid(j)), w_block(d), w_send.at[j], w_recv.at[d], z_peer(j))
    send(w_cols(z), w_block(d), w_send.at[0], w_recv.at[d], x_peer)
    send_st(s_in, own_t, z, f, y_peer)
    send_st(s_in, own_t, z, f, c_peer)
    for j in range(G - 1, 0, -1):
        send_st(s_in, own_t, z, f, z_peer(j))

    R[...] = jnp.zeros_like(R)
    C[...] = jnp.zeros_like(C)
    for copy in locals_:
        copy.wait()
    PH[...] = PH[...] * INV_TURN

    arrive_st(z, fy)
    send_st(s_block(z, fy), t_block(z, fy), z, fy, c_peer)
    for j in range(1, G):
        who = zid(j) * 2 + x
        arrive(w_block(who), w_send.at[0], w_recv.at[who])
        send(w_block(who), w_block(who), w_send.at[G - 1 + j], w_recv.at[who], x_peer)

    def relay_first(j):
        arrive_st(zid(j), f)
        own = (s_block(zid(j), f), t_block(zid(j), f))
        send_st(*own, zid(j), f, y_peer)
        send_st(*own, zid(j), f, c_peer)

    def relay_second(j):
        arrive_st(zid(j), fy)
        send_st(s_block(zid(j), fy), t_block(zid(j), fy), zid(j), fy, c_peer)

    tile_r, tile_c = min(512, rows), min(512, cols)
    col_tiles = cols // tile_c
    steps = (rows // tile_r) * col_tiles

    def compute(base):
        @pl.loop(0, steps)
        def _(t):
            r0 = pl.multiple_of(base + (t // col_tiles) * tile_r, tile_r)
            c0 = pl.multiple_of((t % col_tiles) * tile_c, tile_c)
            here, there = pl.ds(r0, tile_r), pl.ds(c0, tile_c)
            proj = jnp.dot(S[here, :], W[:, there], preferred_element_type=jnp.float32)
            feats = scaled_cos(proj * INV_TURN + PH[:, there], scale).astype(jnp.bfloat16)
            R[here, :] += jnp.dot(feats, RT[there, :], preferred_element_type=jnp.float32)
            C[:, there] += jnp.dot(CT[:, here], feats, preferred_element_type=jnp.float32)

    def r_part(k, yy, cc):
        start = zid(k) * rows + (yy * 2 + cc) * r_rows
        return R.at[pl.ds(pl.multiple_of(start, r_rows), r_rows), :]

    def range_core(k):
        for q, yy in enumerate((1 - y, y)):
            send(r_part(k, yy, 1 - c), RC.at[2 * k + q], rc_send.at[2 * k + q],
                 rc_recv.at[2 * k + q], c_peer)

    def range_y(k):
        arrive(RC.at[2 * k], rc_send.at[0], rc_recv.at[2 * k])
        RS[k] = r_part(k, 1 - y, c)[...] + RC[2 * k]
        send(RS.at[k], RY.at[k], ry_send.at[k], ry_recv.at[k], y_peer)

    def range_z(k):
        arrive(RC.at[2 * k + 1], rc_send.at[0], rc_recv.at[2 * k + 1])
        arrive(RY.at[k], ry_send.at[0], ry_recv.at[k])
        total = r_part(k, y, c)[...] + RC[2 * k + 1] + RY[k]
        if k == 0:
            out_r[...] = total
        else:
            RF[k] = total.astype(RF.dtype)
            send(RF.at[k], RZ.at[k], rz_send.at[k], rz_recv.at[k], z_peer(k))

    if G > 1:
        relay_first(1)
    for j in range(G):
        who = zid(j) * 2 + (1 - x)
        arrive(w_block(who), w_send.at[0], w_recv.at[who])

    for k in range(G):
        if k + 1 < G:
            relay_second(k + 1)
        if k + 2 < G:
            relay_first(k + 2)
        arrive_st(zid(k), fc)
        arrive_st(zid(k), (1 - y) * 2 + (1 - c))
        compute(zid(k) * rows)
        range_core(k)
        if k >= 1:
            range_y(k - 1)
        if k >= 2:
            range_z(k - 2)

    def c_part(j, xx):
        start = (zid(j) * 2 + xx) * c_rows
        return C.at[pl.ds(pl.multiple_of(start, c_rows), c_rows), :]

    order = list(range(1, G)) + [0]
    for j in order:
        send(c_part(j, 1 - x), CX.at[j], cx_send.at[j], cx_recv.at[j], x_peer)
    range_y(G - 1)
    if G >= 2:
        range_z(G - 2)
    for j in order:
        arrive(CX.at[j], cx_send.at[0], cx_recv.at[j])
        total = c_part(j, x)[...] + CX[j]
        if j == 0:
            out_c[:, pl.ds(col0, cols)] = total
        else:
            CS[j] = total.astype(CS.dtype)
            send(CS.at[j], CR.at[j], cz_send.at[j], cz_recv.at[j], z_peer(j))
    range_z(G - 1)

    for j in range(1, G):
        arrive(RZ.at[j], rz_send.at[0], rz_recv.at[j])
        out_r[...] += RZ[j].astype(jnp.float32)
    for j in range(1, G):
        arrive(CR.at[j], cz_send.at[0], cz_recv.at[j])
        source = pl.multiple_of(((z - j + G) % G) * cols, LANES)
        out_c[:, pl.ds(source, cols)] = CR[j].astype(jnp.float32)
    for copy in started:
        copy.wait_send()


def in_kernel(samples, freqs, phases, range_test, corange_test):
    G = lax.axis_size("dp") // 2
    rows, width = samples.shape
    depth, all_cols = freqs.shape
    cols = all_cols // G
    rank = corange_test.shape[0]
    f32, bf16 = jnp.float32, jnp.bfloat16
    scale = math.sqrt(2.0 / (all_cols * 4))
    V, DMA = pltpu.VMEM, pltpu.SemaphoreType.DMA
    block = (rows // 4, rank)
    crow = (rank // (2 * G), cols)
    any_spec = pl.BlockSpec(memory_space=pl.ANY)
    vmem_spec = pl.BlockSpec(memory_space=pltpu.VMEM)
    flops = 2 * G * rows * cols * (4 * width + 2 * rank)
    return pl.pallas_call(
        functools.partial(kernel, G, scale),
        out_shape=(
            jax.ShapeDtypeStruct(block, f32),
            jax.ShapeDtypeStruct((rank // (2 * G), all_cols), f32),
        ),
        in_specs=[any_spec] * 5,
        out_specs=(vmem_spec, vmem_spec),
        scratch_shapes=[
            V((G * rows, 4 * width), bf16),
            V((2 * G * depth, cols), bf16),
            V((1, cols), f32),
            V((cols, rank), bf16),
            V((rank, G * rows), bf16),
            V((G * rows, rank), f32),
            V((rank, cols), f32),
            V((2 * G, *block), f32),
            V((G, *block), f32),
            V((G, *block), WIRE),
            V((G, *block), f32),
            V((G, *block), WIRE),
            V((G, *crow), f32),
            V((G, *crow), WIRE),
            V((G, *crow), WIRE),
            DMA((5,)),
            DMA((2 * G,)), DMA((2 * G,)),
            DMA((4 * G,)), DMA((4 * G,)),
            DMA((4 * G,)), DMA((4 * G,)),
            DMA((2 * G,)), DMA((2 * G,)),
            DMA((G,)), DMA((G,)),
            DMA((G,)), DMA((G,)),
            DMA((G,)), DMA((G,)),
            DMA((G,)), DMA((G,)),
        ],
        compiler_params=pltpu.CompilerParams(
            collective_id=0, has_side_effects=True, vmem_limit_bytes=56 * 2**20
        ),
        cost_estimate=pl.CostEstimate(
            flops=flops, bytes_accessed=2**24, transcendentals=0
        ),
    )(samples, freqs, phases[None, :], range_test, corange_test)


def with_collectives(samples, freqs, phases, range_test, corange_test):
    scale = math.sqrt(2.0 / (freqs.shape[1] * lax.axis_size("feat")))
    projection = jnp.dot(
        lax.all_gather(samples, "feat", axis=1, tiled=True),
        lax.all_gather(freqs, "dp", axis=0, tiled=True),
        preferred_element_type=jnp.float32,
    )
    turns = projection * INV_TURN + phases[None, :] * INV_TURN
    features = scaled_cos(turns, scale).astype(jnp.bfloat16)
    range_sketch = lax.psum_scatter(
        jnp.dot(features, range_test, preferred_element_type=jnp.float32),
        "feat", scatter_dimension=0, tiled=True,
    )
    corange_sketch = lax.psum_scatter(
        jnp.dot(corange_test, features, preferred_element_type=jnp.float32),
        "dp", scatter_dimension=0, tiled=True,
    )
    return (range_sketch, corange_sketch)


def on_device(samples, freqs, phases, range_test, corange_test):
    groups = lax.axis_size("dp") // 2
    fits = (
        lax.axis_size("feat") == 4
        and lax.axis_size("dp") == 2 * groups
        and groups in (2, 4)
        and samples.shape[1] % LANES == 0
    )
    run = in_kernel if fits else with_collectives
    return run(samples, freqs, phases, range_test, corange_test)


def solution(mesh):
    placed = (P("dp", "feat"), P("dp", "feat"), P("feat"), P("feat", None), P(None, "dp"))
    return jax.shard_map(
        on_device,
        mesh=mesh,
        in_specs=placed,
        out_specs=(P(("dp", "feat"), None), P("dp", "feat")),
        check_vma=False,
    )
```

time: 584 us -> 210 us (0.36)
  waiting for transfers between devices: 408 us -> 0 us
  Pallas kernels: 0 us -> 206 us
  matrix products: 143 us -> 0 us
  between operations: 13.8 us -> 0.64 us
  local copies, waits for them, and re-layouts: 14.7 us -> 3.93 us
    all_gather x2 -> x0, waiting for transfers between devices: 252 us -> none  [the longest x1 227 us: on_device(): lax.all_gather(freqs, 'dp', axis=0, tiled=True)]
    pallas_call x0 -> x1, Pallas kernels: none -> 206 us  [in_kernel(): pl.pallas_call(functools.partial(kernel, G, scale), out_shape=(jax.ShapeD...]
    unnamed x5 -> x0, waiting for transfers between devices: 153 us -> none
    dot_general x3 -> x0, matrix products: 143 us -> none  [the longest x1 124 us: on_device(): jnp.dot(gathered, lax.all_gather(freqs, 'dp', axis=0, tiled=True), prefer...]
    unnamed x7 -> x2, local copies, waits for them, and re-layouts: 14.7 us -> 3.93 us
  transfers between devices with their start and end apart: 4 -> 0, of which waited for: 4 -> 0; matrix products, arithmetic and copies ran while one was open for 4% -> 0% of each run, Pallas kernels for 0% -> 0%
where the time goes in v1:
time: 210 us
  Pallas kernels  206 us (98%)
  local copies, waits for them, and re-layouts  3.93 us (2%)
    pallas_call x1, Pallas kernels, in_kernel(): pl.pallas_call(functools.partial(kernel, G, scale), out_shape=(jax.ShapeD...  206 us

profile of v1, /device:TPU:26, one launch (start us, length us, event | category | flops | bytes accessed | tf_op | source)
XLA Modules:
  0.0 210.3 jit_solution(10656251736373648983)
XLA Ops:
  0.6 205.7 %shard_map.68 = (f32[256,256]{1,0:T(8,128)}, f32[32,8192]{1,0:T(8,128)}) custom-call(bf16[1024,256]{1,0:T(8,128)(2,1)} %s_in.1, bf16[128,8192]{1,0:T(8,128)(2,1)} %w_in.1, f32[1,8192]{1,0:T(1,128)} %bitcast.1, bf16[8192,256]{1,0:T(8,128)(2,1)} %rt_in.1, bf16[256,1024]{1,0:T(8,128)(2,1)} %ct_in.1), custom_call_target="tpu_custom_call" | custom-call | flops 25769803776 | bytes 16777216 | tf_op jit(solution)/shard_map/pallas_call | solution.py:262
  206.3 1.7 copy.9
  208.0 2.3 %copy.10 = f32[32,8192]{1,0:T(8,128)} copy(f32[32,8192]{1,0:T(8,128)} %get-tuple-element.5) | data formatting | bytes 2097152

commit v2 on v1

--- a/solution.py
+++ b/solution.py
@@ -11,7 +11,7 @@
 MESH = pl.DeviceIdType.MESH
 INV_TURN = 1.0 / (2.0 * math.pi)
 SIN_TURN = (6.283164044278293, -41.33714236799647, 81.34076878818043, -70.99343236149275)
-WIRE = jnp.float32
+WIRE = jnp.bfloat16
 LANES = 128
 
 

time: 210 us -> 192 us (0.914); the launches traced: 210 us -> 190 us
  Pallas kernels: 206 us -> 185 us
    pallas_call x1, Pallas kernels: 206 us -> 185 us  [in_kernel(): pl.pallas_call(functools.partial(kernel, G, scale), out_shape=(jax.ShapeD...]
where the time goes in v2:
time: 192 us; the launch traced here: 190 us
  Pallas kernels  185 us (96%)
  local copies, waits for them, and re-layouts  3.93 us (2%)
    pallas_call x1, Pallas kernels, in_kernel(): pl.pallas_call(functools.partial(kernel, G, scale), out_shape=(jax.ShapeD...  185 us
    unnamed x2, local copies, waits for them, and re-layouts  3.93 us

profile of v2, /device:TPU:26, one launch (start us, length us, event | category | flops | bytes accessed | tf_op | source)
XLA Modules:
  0.0 189.9 jit_solution(10944062421191261108)
XLA Ops:
  0.6 185.3 %shard_map.68 = (f32[256,256]{1,0:T(8,128)}, f32[32,8192]{1,0:T(8,128)}) custom-call(bf16[1024,256]{1,0:T(8,128)(2,1)} %s_in.1, bf16[128,8192]{1,0:T(8,128)(2,1)} %w_in.1, f32[1,8192]{1,0:T(1,128)} %bitcast.1, bf16[8192,256]{1,0:T(8,128)(2,1)} %rt_in.1, bf16[256,1024]{1,0:T(8,128)(2,1)} %ct_in.1), custom_call_target="tpu_custom_call" | custom-call | flops 25769803776 | bytes 16777216 | tf_op jit(solution)/shard_map/pallas_call | solution.py:262
  186.0 1.7 copy.9
  187.7 2.3 %copy.10 = f32[32,8192]{1,0:T(8,128)} copy(f32[32,8192]{1,0:T(8,128)} %get-tuple-element.5) | data formatting | bytes 2097152
